TPU v7x, 512 devices: a whole 4x4x16 slice. The times are simulated.
512 devices in a mesh: dp: 128 (over x, z_lo, y), mp: 2 (over core), gen: 2 (over z_hi).
Axes of the slice: x: 4, y: 4, z: 16 (z_hi: 2, z_lo: 8; z = z_hi * 8 + z_lo), core: 2. Of those that a mesh axis runs over, the one named last changes fastest.
Arguments:
- fresh_tokens: bfloat16 [32768, 1536], P(('dp', 'gen')), may hold values from -6 to 6
- saved_tokens: bfloat16 [32768, 1536], P('dp'), may hold values from -6 to 6
- cotangents: bfloat16 [2, 32768, 1536], P(None, 'dp', ('mp', 'gen')), may hold values from -20 to 20
- feedback: bfloat16 [2, 128, 1536, 1536], P(None, 'dp', None, ('mp', 'gen')), may hold values from -6 to 6
- start_factors: bfloat16 [2, 1536, 32], P(None, ('mp', 'gen')), may hold values from -6 to 6
Outputs:
- row_basis: float32 [2, 1536, 32], replicated
- col_factors: float32 [2, 1536, 32], P(None, ('mp', 'gen'))
All inputs are finite; a program needn't handle non-finite values.
Results may differ from a plain program's by a relative error of at most 0.0033.
Values may be sent and summed in bfloat16 or wider, within the bound.
A program may use at most 64 MiB of HBM per device.

v0:
```python
import math

import jax
import jax.numpy as jnp
from jax import lax
from jax.sharding import PartitionSpec as P

highest = lax.Precision.HIGHEST


def compensated(tokens, grads, carried):
    grad_sum = lax.dot_general(
        tokens, grads, (((0,), (0,)), ((), ())), preferred_element_type=jnp.float32
    )
    return (grad_sum + carried.astype(jnp.float32)).astype(jnp.bfloat16)


def orthonormal(lower_factor, columns):
    return jax.scipy.linalg.solve_triangular(lower_factor, columns.T, lower=True).T


def compress(matrices, starts):
    power_terms = jnp.stack(
        [
            jnp.dot(matrix, start, preferred_element_type=jnp.float32)
            for matrix, start in zip(matrices, starts)
        ],
        axis=1,
    )
    rows_part = lax.psum(power_terms, ("dp", "mp", "gen"))
    gram_matrix = jnp.einsum("ikr,iks->krs", rows_part, rows_part, precision=highest)
    lower_factor = jnp.linalg.cholesky(gram_matrix)
    ortho_rows = jnp.stack([orthonormal(lower_factor[0], rows_part[:, 0, :])], axis=1)
    coeff_terms = jnp.stack(
        [
            lax.dot_general(
                matrix,
                ortho_rows[:, position, :].astype(jnp.bfloat16),
                (((0,), (0,)), ((), ())),
                preferred_element_type=jnp.float32,
            )
            for position, matrix in enumerate(matrices)
        ],
        axis=1,
    )
    coeffs = lax.psum(coeff_terms, "dp")
    return (ortho_rows, coeffs)


def local(fresh_tokens, saved_tokens, cotangents, feedback, start_factors):
    gathered = lax.all_gather(fresh_tokens, "gen", axis=0, tiled=True)
    layer_inputs = [gathered, saved_tokens]
    count_layers = cotangents.shape[0]
    results = []
    for which in range(count_layers):
        matrix = compensated(layer_inputs[which], cotangents[which], feedback[which, 0])
        results.append(compress([matrix], [start_factors[which]]))
    bases = jnp.concatenate([result[0] for result in results], axis=1)
    coeffs = jnp.concatenate([result[1] for result in results], axis=1)
    row_basis = math.sqrt(bases.shape[0]) * jnp.transpose(bases, (1, 0, 2))
    col_factors = jnp.transpose(coeffs, (1, 0, 2)) / lax.axis_size("dp")
    return (row_basis, col_factors)


def solution(mesh):
    return jax.shard_map(
        local,
        mesh=mesh,
        in_specs=(
            P(("dp", "gen"), None),
            P("dp", None),
            P(None, "dp", ("mp", "gen")),
            P(None, "dp", None, ("mp", "gen")),
            P(None, ("mp", "gen"), None),
        ),
        out_specs=(P(), P(None, ("mp", "gen"), None)),
        check_vma=False,
    )
```

profile of v0, /device:TPU:0, one launch (start us, length us, event | category | flops | bytes accessed | tf_op | source)
XLA Modules:
  0.0 2355.7 jit_solution(10626338235060310586)
XLA Ops:
  7.2 0.0 copy-start
  7.2 0.0 copy-start.4
  7.2 0.0 all-reduce.5.cloned.1.call-start
  7.2 23.2 all_gather.3
  30.4 0.0 copy-done.4
  30.4 0.0 copy-start.3
  30.4 2.0 fusion
  32.5 0.0 copy-done
  32.5 0.0 copy-done.3
  32.5 0.0 copy-start.2
  32.5 0.6 fusion.1
  33.1 0.2 copy-done.2
  33.3 1.1 fusion.14
  34.4 1.1 fusion.12
  35.6 0.0 all-reduce.5.cloned.1.call-update
  35.6 0.0 all-reduce.7.cloned.1.call-start
  35.6 488.0 %all-reduce.5.cloned.1.call-done = (f32[1536,32]{0,1:T(8,128)}, f32[1536,32]{0,1:T(8,128)}) async-done(((f32[1536,32]{0,1:T(8,128)}, f32[1536,32]{0,1:T(8,128)}), (f32[1536,32]{0,1:T(8,128)}, f32[1536,32]{0,1:T(8,128)})) %all-reduce.5.cloned.1.call-update) | async-done | bytes 393232 | tf_op jit(solution)/shard_map/psum | solution.py:30
  523.6 1.3 fusion.31
  524.9 0.0 copy-start.1
  524.9 1.4 fusion.30
  526.3 0.1 copy.8
  526.4 2.9 custom-call.8
  529.3 0.6 compare_reduce_fusion.1
  530.0 0.7 fusion.23
  530.6 3.1 custom-call.9
  533.7 1.3 fusion.6
  535.0 0.9 convolution_bitcast_fusion.1
  535.9 0.1 copy.10
  536.0 2.9 custom-call.10
  539.0 0.6 compare_reduce_fusion
  539.6 0.7 fusion.21
  540.3 2.4 custom-call.11
  542.7 0.0 copy-done.1
  542.7 0.4 fusion.3
  543.1 0.9 convolution_bitcast_fusion
  544.0 0.0 all-reduce.7.cloned.1.call-update
  544.0 0.8 fusion.2
  544.8 1802.6 %all-reduce.7.cloned.1.call-done = (f32[384,1,32]{0,2,1:T(8,128)}, f32[384,1,32]{0,2,1:T(8,128)}) async-done(((f32[384,1,32]{0,2,1:T(8,128)}, f32[384,1,32]{0,2,1:T(8,128)}), (f32[384,1,32]{0,2,1:T(8,128)}, f32[384,1,32]{0,2,1:T(8,128)})) %all-reduce.7.cloned.1.call-update) | async-done | bytes 98320 | tf_op jit(solution)/shard_map/psum | solution.py:46
  2347.4 1.5 fusion.11
  (4 shorter events, 0.1 us)
Async XLA Ops:
  7.2 25.3 %copy-start = (bf16[256,1536]{1,0:T(8,128)(2,1)S(1)}, bf16[256,1536]{1,0:T(8,128)(2,1)}, u32[]{:S(2)}) copy-start(bf16[256,1536]{1,0:T(8,128)(2,1)} %param.9) | copy-start | bytes 2359300
  7.2 23.2 copy-start.4
  7.2 516.4 %all-reduce.5.cloned.1.call-start = ((), (), s32[]{:S(2)}) async-start(), calls=%async_computation | async-start | bytes 786432 | tf_op jit(solution)/shard_map/psum | solution.py:30
  30.4 2.0 copy-start.3
  32.5 0.8 copy-start.2
  35.6 2311.8 %all-reduce.7.cloned.1.call-start = ((), (), s32[]{:S(2)}) async-start(), calls=%async_computation.1 | async-start | bytes 196608 | tf_op jit(solution)/shard_map/psum | solution.py:46
  524.9 17.8 copy-start.1
Sparse Core Ops, SparseCore 0:
  35.7 487.8 all-reduce.4
  544.2 1803.1 all-reduce.6
where the time goes:
time: 2360 us
  waiting for transfers between devices  2290 us (97%)
    psum x1, waiting for transfers between devices, compress(): coeffs = lax.psum(coeff_terms, 'dp')  1800 us
    psum x1, waiting for transfers between devices, compress(): rows_part = lax.psum(power_terms, ('dp', 'mp', 'gen'))  488 us
  transfers between devices with their start and end apart: 2, of which 2 were waited for; matrix products, arithmetic and copies ran while one was open for 0% of the time, Pallas kernels for 0%

commit v1 on v0

v1 whole, which is shorter than its diff:
```python
import math

import jax
import jax.numpy as jnp
from jax import lax
from jax.experimental import pallas as pl
from jax.experimental.pallas import tpu as pltpu
from jax.sharding import PartitionSpec as P

MESH = pl.DeviceIdType.MESH
HIGHEST = lax.Precision.HIGHEST
f32, bf16 = jnp.float32, jnp.bfloat16
NN = (((1,), (0,)), ((), ()))
NT = (((1,), (1,)), ((), ()))


def dot(a, b, dims, precision=None):
    return lax.dot_general(a, b, dims, precision=precision, preferred_element_type=f32)


def halves(value):
    high = value.astype(bf16)
    low = (value - high.astype(f32)).astype(bf16)
    return jnp.concatenate([high, low], axis=0)


def fold(value):
    rows = value.shape[0] // 2
    return value[:rows] + value[rows:]


def inverse_factor(gram):
    n = gram.shape[0]
    rows = lax.broadcasted_iota(jnp.int32, (n, n), 0)
    cols = lax.broadcasted_iota(jnp.int32, (n, n), 1)
    left, right = gram, jnp.where(rows == cols, 1.0, 0.0).astype(f32)
    for j in range(n - 1):
        factor = left[:, j : j + 1] / left[j : j + 1, j : j + 1]
        factor = jnp.where(rows > j, factor, 0.0)
        left, right = left - factor * left[j : j + 1, :], right - factor * right[j : j + 1, :]
    pivots = jnp.sum(jnp.where(rows == cols, left, 0.0), axis=1, keepdims=True)
    return right / jnp.sqrt(pivots)


def wait_bytes(ref, sem):
    pltpu.make_async_copy(ref, ref, sem).wait()


def kernel(
    t0_in, t1_in, g_in, f_in, s_in, rb_out, cf_out,
    t0, t1, g, f, s, u, u_got, g_got, part, rsb, zbuf, pfull, mpart, rs2b, acc2, z2b, mfull, linv, rb, cf,
    load_sem, store_sem, u_sem, g_sem, rs_send, rs_recv, z_sem, ag_send, ag_recv, rs2_sem, z2_sem, ag2_sem,
):
    rem, div = lax.rem, lax.div
    dp, c, gen = lax.axis_index("dp"), lax.axis_index("mp"), lax.axis_index("gen")
    x, y, zlo = div(dp, 32), rem(dp, 4), rem(div(dp, 4), 8)
    z = gen * 8 + zlo
    me = x * 4 + y

    def device(x2, y2, z2, c2):
        return (x2 * 32 + rem(z2, 8) * 4 + y2, c2, div(z2, 8))

    partner = device(x, y, rem(z + 8, 16), c)

    def z_step(i):
        h = div(i + 1, 2)
        return 8 + h * (1 - 2 * rem(i, 2))

    def xy_step(i):
        return rem(2 + div(i, 4), 4), rem(2 + i, 4)

    def loop(n, body):
        def step(i, carry):
            body(i)
            return carry

        lax.fori_loop(0, n, step, 0)

    barrier = pltpu.get_barrier_semaphore()

    def hello_z(i):
        pl.semaphore_signal(
            barrier, inc=1, device_id=device(x, y, rem(z + z_step(i), 16), c), device_id_type=MESH
        )

    def hello_xy(i):
        dx, dy = xy_step(div(i, 2))
        dc = rem(i, 2)

        @pl.when(dx + dy + dc != 0)
        def _():
            pl.semaphore_signal(
                barrier, inc=1,
                device_id=device(rem(x + dx, 4), rem(y + dy, 4), z, rem(c + dc, 2)), device_id_type=MESH,
            )

    loads = [
        pltpu.make_async_copy(s_in, s, load_sem.at[0]),
        pltpu.make_async_copy(g_in.at[0], g.at[0], load_sem.at[1]),
        pltpu.make_async_copy(g_in.at[1], g.at[1], load_sem.at[2]),
        pltpu.make_async_copy(t1_in, t1, load_sem.at[3]),
        pltpu.make_async_copy(f_in.at[1], f.at[1], load_sem.at[4]),
        pltpu.make_async_copy(f_in.at[0], f.at[0], load_sem.at[5]),
        pltpu.make_async_copy(t0_in, t0, load_sem.at[6]),
    ]
    loop(15, hello_z)
    for load in loads:
        load.start()
    loop(32, hello_xy)

    loads[0].wait()
    loads[1].wait()
    u_all = dot(s[0], g[0], NT)
    u[0] = u_all[:, :128]
    u[1] = u_all[:, 128:]
    loads[2].wait()
    u1 = halves(dot(s[1], g[1], NT))
    loads[3].wait()
    loads[4].wait()
    for q in range(4):
        span = slice(384 * q, 384 * q + 384)
        block = fold(dot(u1, t1[:, span], NN)) + dot(s[1], f[1, span, :], NT)
        part[1, 4 * q : 4 * q + 4] = block.reshape(4, 8, 384)
    loads[5].wait()
    for q in range(4):
        span = slice(384 * q, 384 * q + 384)
        part[0, 4 * q : 4 * q + 4] = dot(s[0], f[0, span, :], NT).reshape(4, 8, 384)

    pl.semaphore_wait(barrier, 46)

    u_copy = pltpu.make_async_remote_copy(
        src_ref=u.at[1 - gen], dst_ref=u_got, send_sem=u_sem.at[0], recv_sem=u_sem.at[1],
        device_id=partner, device_id_type=MESH,
    )
    u_copy.start()

    def send_part(layer):
        def body(i):
            dx, dy = xy_step(i)
            x2, y2 = rem(x + dx, 4), rem(y + dy, 4)
            slot = (dx * 4 + dy) * 2 + rem(c + layer, 2)

            @pl.when(slot != 0)
            def _():
                pltpu.make_async_remote_copy(
                    src_ref=part.at[layer, x2 * 4 + y2], dst_ref=rsb.at[slot],
                    send_sem=rs_send.at[layer], recv_sem=rs_recv,
                    device_id=device(x2, y2, z, layer), device_id_type=MESH,
                ).start()

        loop(16, body)

    def reduce_part(layer):
        wait_bytes(rsb.at[pl.ds(1, 31)], rs_recv)
        total = part[layer, me]
        for slot in range(1, 32):
            total = total + rsb[slot]
        zbuf[z] = total

        def body(i):
            pltpu.make_async_remote_copy(
                src_ref=zbuf.at[z], dst_ref=zbuf.at[z], send_sem=z_sem.at[0], recv_sem=z_sem.at[1],
                device_id=device(x, y, rem(z + z_step(i), 16), c), device_id_type=MESH,
            ).start()

        loop(15, body)

    def gather_power(layer):
        wait_bytes(zbuf.at[pl.ds(0, 15)], z_sem.at[1])
        total = zbuf[0]
        for slot in range(1, 16):
            total = total + zbuf[slot]
        pfull[layer, me] = total

        def body(i):
            dx, dy = xy_step(div(i, 2))
            dc = rem(i, 2)

            @pl.when(dx + dy + dc != 0)
            def _():
                pltpu.make_async_remote_copy(
                    src_ref=pfull.at[layer, me], dst_ref=pfull.at[layer, me],
                    send_sem=ag_send, recv_sem=ag_recv.at[layer],
                    device_id=device(rem(x + dx, 4), rem(y + dy, 4), z, rem(c + dc, 2)), device_id_type=MESH,
                ).start()

        loop(32, body)

    def wait_power(layer):
        @pl.when(c == layer)
        def _():
            wait_bytes(pfull.at[layer, pl.ds(0, 15)], ag_recv.at[layer])

        @pl.when(c != layer)
        def _():
            wait_bytes(pfull.at[layer, pl.ds(0, 16)], ag_recv.at[layer])

    def power_block(layer, q):
        return pfull[layer, 4 * q : 4 * q + 4].reshape(32, 384)

    send_part(1)
    g_copy = pltpu.make_async_remote_copy(
        src_ref=g.at[0, pl.ds(pl.multiple_of((1 - gen) * 128, 128), 128)], dst_ref=g_got,
        send_sem=g_sem.at[0], recv_sem=g_sem.at[1], device_id=partner, device_id_type=MESH,
    )
    g_copy.start()

    @pl.when(c == 1)
    def _():
        reduce_part(1)

    loads[6].wait()
    u_copy.wait()
    u0 = halves(u[gen] + u_got[...])
    for q in range(4):
        span = slice(384 * q, 384 * q + 384)
        block = fold(dot(u0, t0[:, span], NN)).reshape(4, 8, 384)
        part[0, 4 * q : 4 * q + 4] = part[0, 4 * q : 4 * q + 4] + block
    send_part(0)

    @pl.when(c == 1)
    def _():
        gather_power(1)

    @pl.when(c == 0)
    def _():
        reduce_part(0)
        gather_power(0)

    def products(layer, tokens):
        direct, by_token = None, None
        for q in range(4):
            span = slice(384 * q, 384 * q + 384)
            block = halves(power_block(layer, q))
            one = dot(block, f[layer, span, :], NN)
            two = dot(block, tokens[:, span], NT)
            direct = one if direct is None else direct + one
            by_token = two if by_token is None else by_token + two
        return fold(direct), halves(fold(by_token))

    def put(place, value):
        for q in range(3):
            mpart[4 * q : 4 * q + 4, place] = value[:, 128 * q : 128 * q + 128].reshape(4, 8, 128)

    def factorize(layer):
        gram = None
        for q in range(4):
            block = power_block(layer, q)
            one = dot(block, block, NT, HIGHEST)
            gram = one if gram is None else gram + one
        inverse = inverse_factor(gram)
        linv[layer] = inverse
        scaled = inverse * math.sqrt(1536)
        for q in range(4):
            rb[layer, :, 384 * q : 384 * q + 384] = dot(scaled, power_block(layer, q), NN, HIGHEST)

    rb_stores = [pltpu.make_async_copy(rb.at[i], rb_out.at[i], store_sem.at[i]) for i in range(2)]

    wait_power(1)
    direct, by_token = products(1, t1)
    put(1, direct + fold(dot(by_token, g[1], NN)))
    factorize(1)
    rb_stores[1].start()

    g_copy.wait()
    wait_power(0)
    direct, by_token = products(0, t0)
    own_rows = g[0, pl.ds(pl.multiple_of(gen * 128, 128), 128), :]
    put(0, direct + fold(dot(by_token, own_rows, NN)))
    put(2, fold(dot(by_token, g_got[...], NN)))

    def send_coeffs(i):
        dx, dy = xy_step(i)
        x2, y2 = rem(x + dx, 4), rem(y + dy, 4)

        @pl.when((dx + dy != 0) & (x2 < 3))
        def _():
            pltpu.make_async_remote_copy(
                src_ref=mpart.at[x2 * 4 + y2], dst_ref=rs2b.at[dx * 4 + dy],
                send_sem=rs2_sem.at[0], recv_sem=rs2_sem.at[1],
                device_id=device(x2, y2, z, c), device_id_type=MESH,
            ).start()

    loop(16, send_coeffs)
    factorize(0)
    rb_stores[0].start()

    @pl.when(x < 3)
    def _():
        wait_bytes(rs2b.at[pl.ds(1, 15)], rs2_sem.at[1])
        total = mpart[me]
        for slot in range(1, 16):
            total = total + rs2b[slot]
        acc2[...] = total
        z2b[z] = total[:2]

        def body(i):
            z2 = rem(z + z_step(i), 16)
            where = device(x, y, z2, c)

            @pl.when(div(z2, 8) == gen)
            def _():
                pltpu.make_async_remote_copy(
                    src_ref=acc2.at[pl.ds(0, 2)], dst_ref=z2b.at[z],
                    send_sem=z2_sem.at[0], recv_sem=z2_sem.at[1], device_id=where, device_id_type=MESH,
                ).start()

            @pl.when(div(z2, 8) != gen)
            def _():
                pltpu.make_async_remote_copy(
                    src_ref=acc2.at[2], dst_ref=z2b.at[z, 0],
                    send_sem=z2_sem.at[2], recv_sem=z2_sem.at[3], device_id=where, device_id_type=MESH,
                ).start()

        loop(15, body)
        wait_bytes(z2b.at[pl.ds(0, 7)], z2_sem.at[1])
        wait_bytes(z2b.at[pl.ds(0, 4)], z2_sem.at[3])
        first = z2b[0, 0]
        for slot in range(1, 16):
            first = first + z2b[slot, 0]
        second = z2b[gen * 8, 1]
        for slot in range(1, 8):
            second = second + z2b[gen * 8 + slot, 1]
        mfull[me, 0] = first
        mfull[me, 1] = second

        def share(i):
            dx, dy = xy_step(i)

            @pl.when(dx + dy != 0)
            def _():
                pltpu.make_async_remote_copy(
                    src_ref=mfull.at[me], dst_ref=mfull.at[me],
                    send_sem=ag2_sem.at[0], recv_sem=ag2_sem.at[1],
                    device_id=device(rem(x + dx, 4), rem(y + dy, 4), z, c), device_id_type=MESH,
                ).start()

        loop(16, share)
        wait_bytes(mfull.at[pl.ds(0, 11)], ag2_sem.at[1])

    @pl.when(x == 3)
    def _():
        wait_bytes(mfull.at[pl.ds(0, 12)], ag2_sem.at[1])

    for layer in range(2):
        scaled = linv[layer] * (1.0 / 128.0)
        for q in range(3):
            block = mfull[4 * q : 4 * q + 4, layer].reshape(32, 128)
            cf[layer, :, 128 * q : 128 * q + 128] = dot(scaled, block, NN, HIGHEST)
    cf_store = pltpu.make_async_copy(cf, cf_out, store_sem.at[2])
    cf_store.start()

    for layer in range(2):

        @pl.when(c == layer)
        def _():
            wait_bytes(part.at[layer, pl.ds(0, 15)], rs_send.at[layer])

        @pl.when(c != layer)
        def _():
            wait_bytes(part.at[layer, pl.ds(0, 16)], rs_send.at[layer])

    wait_bytes(zbuf.at[pl.ds(0, 15)], z_sem.at[0])
    wait_bytes(rsb.at[pl.ds(0, 31)], ag_send)

    @pl.when(x < 3)
    def _():
        wait_bytes(mpart.at[pl.ds(0, 11)], rs2_sem.at[0])
        wait_bytes(z2b.at[pl.ds(0, 7)], z2_sem.at[0])
        wait_bytes(z2b.at[pl.ds(0, 4)], z2_sem.at[2])
        wait_bytes(rs2b.at[pl.ds(0, 10)], ag2_sem.at[0])

    @pl.when(x == 3)
    def _():
        wait_bytes(mpart.at[pl.ds(0, 12)], rs2_sem.at[0])

    rb_stores[0].wait()
    rb_stores[1].wait()
    cf_store.wait()


def local(fresh_tokens, saved_tokens, cotangents, feedback, start_factors):
    anywhere = pl.BlockSpec(memory_space=pl.ANY)
    vmem, dma = pltpu.VMEM, pltpu.SemaphoreType.DMA
    rb, cf = pl.pallas_call(
        kernel,
        out_shape=(
            jax.ShapeDtypeStruct((2, 32, 1536), f32),
            jax.ShapeDtypeStruct((2, 32, 384), f32),
        ),
        in_specs=[anywhere] * 5,
        out_specs=(anywhere, anywhere),
        scratch_shapes=[
            vmem((128, 1536), bf16),
            vmem((256, 1536), bf16),
            vmem((2, 256, 384), bf16),
            vmem((2, 1536, 384), bf16),
            vmem((2, 32, 384), bf16),
            vmem((2, 32, 128), f32),
            vmem((32, 128), f32),
            vmem((128, 384), bf16),
            vmem((2, 16, 8, 384), f32),
            vmem((32, 8, 384), f32),
            vmem((16, 8, 384), f32),
            vmem((2, 16, 8, 384), f32),
            vmem((12, 3, 8, 128), f32),
            vmem((16, 3, 8, 128), f32),
            vmem((3, 8, 128), f32),
            vmem((16, 2, 8, 128), f32),
            vmem((12, 2, 8, 128), f32),
            vmem((2, 32, 32), f32),
            vmem((2, 32, 1536), f32),
            vmem((2, 32, 384), f32),
            dma((7,)),
            dma((3,)),
            dma((2,)),
            dma((2,)),
            dma((2,)),
            dma,
            dma((2,)),
            dma,
            dma((2,)),
            dma((2,)),
            dma((4,)),
            dma((2,)),
        ],
        compiler_params=pltpu.CompilerParams(
            collective_id=0, has_side_effects=True, vmem_limit_bytes=60 * 2**20
        ),
        cost_estimate=pl.CostEstimate(flops=10**9, bytes_accessed=5 * 10**6, transcendentals=0),
        name="compress",
    )(
        fresh_tokens,
        saved_tokens,
        cotangents,
        feedback.reshape(2, 1536, 384),
        jnp.transpose(start_factors, (0, 2, 1)),
    )
    return jnp.transpose(rb, (0, 2, 1)), jnp.transpose(cf, (0, 2, 1))


def solution(mesh):
    return jax.shard_map(
        local,
        mesh=mesh,
        in_specs=(
            P(("dp", "gen"), None),
            P("dp", None),
            P(None, "dp", ("mp", "gen")),
            P(None, "dp", None, ("mp", "gen")),
            P(None, ("mp", "gen"), None),
        ),
        out_specs=(P(), P(None, ("mp", "gen"), None)),
        check_vma=False,
    )
```

time: 2360 us -> 72.8 us (0.03)
  the two profiles are of different devices: /device:TPU:0 before, /device:TPU:2 now
where the time goes in v1:
time: 72.8 us; the launch traced here: 72.6 us
  Pallas kernels  68.7 us (94%)
  local copies, waits for them, and re-layouts  3.31 us (5%)
    pallas_call x1, Pallas kernels, local(): pl.pallas_call(kernel, out_shape=(jax.ShapeDtypeStruct((2, 32, 1536), f32...  68.7 us
    unnamed x2, local copies, waits for them, and re-layouts  3.31 us

profile of v1, /device:TPU:2, one launch (start us, length us, event | category | flops | bytes accessed | tf_op | source)
XLA Modules:
  0.0 72.6 jit_solution(13788721731408960609)
XLA Ops:
  0.6 68.7 %compress.1 = (f32[2,32,1536]{2,1,0:T(8,128)}, f32[2,32,384]{2,1,0:T(8,128)}) custom-call(bf16[128,1536]{1,0:T(8,128)(2,1)} %t0_in.1, bf16[256,1536]{1,0:T(8,128)(2,1)} %t1_in.1, bf16[2,256,384]{2,1,0:T(8,128)(2,1)} %g_in.1, bf16[2,1536,384]{2,1,0:T(8,128)(2,1)} %bitcast.4, bf16[2,32,384]{2,1,0:T(8,128)(2,1)} %bitcast.7), custom_call_target="tpu_custom_call" | custom-call | flops 1000000000 | bytes 5000000 | tf_op jit(solution)/shard_map/compress/pallas_call | solution.py:385
  69.3 1.8 %copy.9 = f32[2,1536,32]{1,2,0:T(8,128)} copy(f32[2,1536,32]{1,2,0:T(8,128)} %bitcast.5) | data formatting | bytes 786432
  71.1 1.5 %copy.10 = f32[2,384,32]{1,2,0:T(8,128)} copy(f32[2,384,32]{1,2,0:T(8,128)} %bitcast.6) | data formatting | bytes 196608

commit v2 on v1

--- a/solution.py
+++ b/solution.py
@@ -12,6 +12,11 @@
 f32, bf16 = jnp.float32, jnp.bfloat16
 NN = (((1,), (0,)), ((), ()))
 NT = (((1,), (1,)), ((), ()))
+XY_STEPS = sorted(
+    [(dx, dy) for dx in range(4) for dy in range(4) if dx + dy > 0],
+    key=lambda step: -sum(min(d, 4 - d) for d in step),
+)
+Z_STEPS = sorted(range(1, 16), key=lambda d: -min(d, 16 - d))
 
 
 def dot(a, b, dims, precision=None):
@@ -56,43 +61,25 @@
     x, y, zlo = div(dp, 32), rem(dp, 4), rem(div(dp, 4), 8)
     z = gen * 8 + zlo
     me = x * 4 + y
-
-    def device(x2, y2, z2, c2):
-        return (x2 * 32 + rem(z2, 8) * 4 + y2, c2, div(z2, 8))
-
-    partner = device(x, y, rem(z + 8, 16), c)
-
-    def z_step(i):
-        h = div(i + 1, 2)
-        return 8 + h * (1 - 2 * rem(i, 2))
-
-    def xy_step(i):
-        return rem(2 + div(i, 4), 4), rem(2 + i, 4)
-
-    def loop(n, body):
-        def step(i, carry):
-            body(i)
-            return carry
-
-        lax.fori_loop(0, n, step, 0)
-
-    barrier = pltpu.get_barrier_semaphore()
-
-    def hello_z(i):
-        pl.semaphore_signal(
-            barrier, inc=1, device_id=device(x, y, rem(z + z_step(i), 16), c), device_id_type=MESH
-        )
-
-    def hello_xy(i):
-        dx, dy = xy_step(div(i, 2))
-        dc = rem(i, 2)
-
-        @pl.when(dx + dy + dc != 0)
-        def _():
-            pl.semaphore_signal(
-                barrier, inc=1,
-                device_id=device(rem(x + dx, 4), rem(y + dy, 4), z, rem(c + dc, 2)), device_id_type=MESH,
-            )
+    xs = [x] + [rem(x + d, 4) for d in range(1, 4)]
+    ys = [y] + [rem(y + d, 4) for d in range(1, 4)]
+    cs = [c, 1 - c]
+    column = zlo * 4
+
+    def plane(dx, dy, core):
+        return (xs[dx] * 32 + column + ys[dy], core, gen)
+
+    def along(dz):
+        other = rem(z + dz, 16)
+        return (x * 32 + rem(other, 8) * 4 + y, c, div(other, 8))
+
+    partner = (dp, c, 1 - gen)
+
+    def send(src, dst, send_sem, recv_sem, device):
+        pltpu.make_async_remote_copy(
+            src_ref=src, dst_ref=dst, send_sem=send_sem, recv_sem=recv_sem,
+            device_id=device, device_id_type=MESH,
+        ).start()
 
     loads = [
         pltpu.make_async_copy(s_in, s, load_sem.at[0]),
@@ -103,16 +90,35 @@
         pltpu.make_async_copy(f_in.at[0], f.at[0], load_sem.at[5]),
         pltpu.make_async_copy(t0_in, t0, load_sem.at[6]),
     ]
-    loop(15, hello_z)
     for load in loads:
         load.start()
-    loop(32, hello_xy)
+
+    barrier = pltpu.get_barrier_semaphore()
+    peers = [along(dz) for dz in Z_STEPS] + [plane(*step, cs[k]) for step in XY_STEPS for k in range(2)]
+    for peer in peers + [plane(0, 0, cs[1])]:
+        pl.semaphore_signal(barrier, inc=1, device_id=peer, device_id_type=MESH)
 
     loads[0].wait()
     loads[1].wait()
     u_all = dot(s[0], g[0], NT)
     u[0] = u_all[:, :128]
     u[1] = u_all[:, 128:]
+    u_copy = pltpu.make_async_remote_copy(
+        src_ref=u.at[1 - gen], dst_ref=u_got, send_sem=u_sem.at[0], recv_sem=u_sem.at[1],
+        device_id=partner, device_id_type=MESH,
+    )
+
+    g_copy = pltpu.make_async_remote_copy(
+        src_ref=g.at[0, pl.ds(pl.multiple_of((1 - gen) * 128, 128), 128)], dst_ref=g_got,
+        send_sem=g_sem.at[0], recv_sem=g_sem.at[1], device_id=partner, device_id_type=MESH,
+    )
+
+    @pl.when(gen == 1)
+    def _():
+        pl.semaphore_wait(barrier, 46)
+        u_copy.start()
+        g_copy.start()
+
     loads[2].wait()
     u1 = halves(dot(s[1], g[1], NT))
     loads[3].wait()
@@ -125,30 +131,25 @@
     for q in range(4):
         span = slice(384 * q, 384 * q + 384)
         part[0, 4 * q : 4 * q + 4] = dot(s[0], f[0, span, :], NT).reshape(4, 8, 384)
-
-    pl.semaphore_wait(barrier, 46)
-
-    u_copy = pltpu.make_async_remote_copy(
-        src_ref=u.at[1 - gen], dst_ref=u_got, send_sem=u_sem.at[0], recv_sem=u_sem.at[1],
-        device_id=partner, device_id_type=MESH,
-    )
-    u_copy.start()
+    loads[6].wait()
+
+    @pl.when(gen == 0)
+    def _():
+        pl.semaphore_wait(barrier, 46)
+        u_copy.start()
+        g_copy.start()
 
     def send_part(layer):
-        def body(i):
-            dx, dy = xy_step(i)
-            x2, y2 = rem(x + dx, 4), rem(y + dy, 4)
-            slot = (dx * 4 + dy) * 2 + rem(c + layer, 2)
-
-            @pl.when(slot != 0)
-            def _():
-                pltpu.make_async_remote_copy(
-                    src_ref=part.at[layer, x2 * 4 + y2], dst_ref=rsb.at[slot],
-                    send_sem=rs_send.at[layer], recv_sem=rs_recv,
-                    device_id=device(x2, y2, z, layer), device_id_type=MESH,
-                ).start()
-
-        loop(16, body)
+        other = rem(c + layer, 2)
+        for dx, dy in XY_STEPS:
+            send(
+                part.at[layer, xs[dx] * 4 + ys[dy]], rsb.at[(dx * 4 + dy) * 2 + other],
+                rs_send.at[layer], rs_recv, plane(dx, dy, layer),
+            )
+
+        @pl.when(other == 1)
+        def _():
+            send(part.at[layer, me], rsb.at[1], rs_send.at[layer], rs_recv, plane(0, 0, layer))
 
     def reduce_part(layer):
         wait_bytes(rsb.at[pl.ds(1, 31)], rs_recv)
@@ -156,14 +157,8 @@
         for slot in range(1, 32):
             total = total + rsb[slot]
         zbuf[z] = total
-
-        def body(i):
-            pltpu.make_async_remote_copy(
-                src_ref=zbuf.at[z], dst_ref=zbuf.at[z], send_sem=z_sem.at[0], recv_sem=z_sem.at[1],
-                device_id=device(x, y, rem(z + z_step(i), 16), c), device_id_type=MESH,
-            ).start()
-
-        loop(15, body)
+        for dz in Z_STEPS:
+            send(zbuf.at[z], zbuf.at[z], z_sem.at[0], z_sem.at[1], along(dz))
 
     def gather_power(layer):
         wait_bytes(zbuf.at[pl.ds(0, 15)], z_sem.at[1])
@@ -171,20 +166,13 @@
         for slot in range(1, 16):
             total = total + zbuf[slot]
         pfull[layer, me] = total
-
-        def body(i):
-            dx, dy = xy_step(div(i, 2))
-            dc = rem(i, 2)
-
-            @pl.when(dx + dy + dc != 0)
-            def _():
-                pltpu.make_async_remote_copy(
-                    src_ref=pfull.at[layer, me], dst_ref=pfull.at[layer, me],
-                    send_sem=ag_send, recv_sem=ag_recv.at[layer],
-                    device_id=device(rem(x + dx, 4), rem(y + dy, 4), z, rem(c + dc, 2)), device_id_type=MESH,
-                ).start()
-
-        loop(32, body)
+        for dx, dy in XY_STEPS + [(0, 0)]:
+            for k in range(2):
+                if dx + dy + k > 0:
+                    send(
+                        pfull.at[layer, me], pfull.at[layer, me],
+                        ag_send, ag_recv.at[layer], plane(dx, dy, cs[k]),
+                    )
 
     def wait_power(layer):
         @pl.when(c == layer)
@@ -199,17 +187,11 @@
         return pfull[layer, 4 * q : 4 * q + 4].reshape(32, 384)
 
     send_part(1)
-    g_copy = pltpu.make_async_remote_copy(
-        src_ref=g.at[0, pl.ds(pl.multiple_of((1 - gen) * 128, 128), 128)], dst_ref=g_got,
-        send_sem=g_sem.at[0], recv_sem=g_sem.at[1], device_id=partner, device_id_type=MESH,
-    )
-    g_copy.start()
-
-    @pl.when(c == 1)
+
+    @pl.when((c == 1) & (gen == 1))
     def _():
         reduce_part(1)
 
-    loads[6].wait()
     u_copy.wait()
     u0 = halves(u[gen] + u_got[...])
     for q in range(4):
@@ -220,6 +202,11 @@
 
     @pl.when(c == 1)
     def _():
+
+        @pl.when(gen == 0)
+        def _():
+            reduce_part(1)
+
         gather_power(1)
 
     @pl.when(c == 0)
@@ -269,19 +256,15 @@
     put(0, direct + fold(dot(by_token, own_rows, NN)))
     put(2, fold(dot(by_token, g_got[...], NN)))
 
-    def send_coeffs(i):
-        dx, dy = xy_step(i)
-        x2, y2 = rem(x + dx, 4), rem(y + dy, 4)
-
-        @pl.when((dx + dy != 0) & (x2 < 3))
-        def _():
-            pltpu.make_async_remote_copy(
-                src_ref=mpart.at[x2 * 4 + y2], dst_ref=rs2b.at[dx * 4 + dy],
-                send_sem=rs2_sem.at[0], recv_sem=rs2_sem.at[1],
-                device_id=device(x2, y2, z, c), device_id_type=MESH,
-            ).start()
-
-    loop(16, send_coeffs)
+    for dx, dy in XY_STEPS:
+
+        @pl.when(xs[dx] < 3)
+        def _():
+            send(
+                mpart.at[xs[dx] * 4 + ys[dy]], rs2b.at[dx * 4 + dy],
+                rs2_sem.at[0], rs2_sem.at[1], plane(dx, dy, c),
+            )
+
     factorize(0)
     rb_stores[0].start()
 
@@ -294,25 +277,17 @@
         acc2[...] = total
         z2b[z] = total[:2]
 
-        def body(i):
-            z2 = rem(z + z_step(i), 16)
-            where = device(x, y, z2, c)
-
-            @pl.when(div(z2, 8) == gen)
+        for dz in Z_STEPS:
+            where = along(dz)
+
+            @pl.when(where[2] == gen)
             def _():
-                pltpu.make_async_remote_copy(
-                    src_ref=acc2.at[pl.ds(0, 2)], dst_ref=z2b.at[z],
-                    send_sem=z2_sem.at[0], recv_sem=z2_sem.at[1], device_id=where, device_id_type=MESH,
-                ).start()
-
-            @pl.when(div(z2, 8) != gen)
+                send(acc2.at[pl.ds(0, 2)], z2b.at[z], z2_sem.at[0], z2_sem.at[1], where)
+
+            @pl.when(where[2] != gen)
             def _():
-                pltpu.make_async_remote_copy(
-                    src_ref=acc2.at[2], dst_ref=z2b.at[z, 0],
-                    send_sem=z2_sem.at[2], recv_sem=z2_sem.at[3], device_id=where, device_id_type=MESH,
-                ).start()
-
-        loop(15, body)
+                send(acc2.at[2], z2b.at[z, 0], z2_sem.at[2], z2_sem.at[3], where)
+
         wait_bytes(z2b.at[pl.ds(0, 7)], z2_sem.at[1])
         wait_bytes(z2b.at[pl.ds(0, 4)], z2_sem.at[3])
         first = z2b[0, 0]
@@ -324,18 +299,8 @@
         mfull[me, 0] = first
         mfull[me, 1] = second
 
-        def share(i):
-            dx, dy = xy_step(i)
-
-            @pl.when(dx + dy != 0)
-            def _():
-                pltpu.make_async_remote_copy(
-                    src_ref=mfull.at[me], dst_ref=mfull.at[me],
-                    send_sem=ag2_sem.at[0], recv_sem=ag2_sem.at[1],
-                    device_id=device(rem(x + dx, 4), rem(y + dy, 4), z, c), device_id_type=MESH,
-                ).start()
-
-        loop(16, share)
+        for step in XY_STEPS:
+            send(mfull.at[me], mfull.at[me], ag2_sem.at[0], ag2_sem.at[1], plane(*step, c))
         wait_bytes(mfull.at[pl.ds(0, 11)], ag2_sem.at[1])
 
     @pl.when(x == 3)
@@ -377,6 +342,17 @@
     rb_stores[0].wait()
     rb_stores[1].wait()
     cf_store.wait()
+
+
+def write_out(rb, cf, rb_out, cf_out, sem):
+    copies = [
+        pltpu.make_async_copy(rb, rb_out, sem.at[0]),
+        pltpu.make_async_copy(cf, cf_out, sem.at[1]),
+    ]
+    for copy in copies:
+        copy.start()
+    for copy in copies:
+        copy.wait()
 
 
 def local(fresh_tokens, saved_tokens, cotangents, feedback, start_factors):
@@ -436,6 +412,17 @@
         feedback.reshape(2, 1536, 384),
         jnp.transpose(start_factors, (0, 2, 1)),
     )
+    rb, cf = pl.pallas_call(
+        write_out,
+        out_shape=(
+            jax.ShapeDtypeStruct((2, 32, 1536), f32),
+            jax.ShapeDtypeStruct((2, 32, 384), f32),
+        ),
+        in_specs=[pl.BlockSpec(memory_space=vmem)] * 2,
+        out_specs=(anywhere, anywhere),
+        scratch_shapes=[dma((2,))],
+        name="write_out",
+    )(rb, cf)
     return jnp.transpose(rb, (0, 2, 1)), jnp.transpose(cf, (0, 2, 1))
 
 

time: 72.8 us -> 67.3 us (0.924)
  the two profiles are of different devices: /device:TPU:2 before, /device:TPU:8 now
where the time goes in v2:
time: 67.3 us; the launch traced here: 67.1 us
  Pallas kernels  66.5 us (99%)
    pallas_call x1, Pallas kernels, local(): pl.pallas_call(kernel, out_shape=(jax.ShapeDtypeStruct((2, 32, 1536), f32...  64.7 us
    pallas_call x1, Pallas kernels, local(): pl.pallas_call(write_out, out_shape=(jax.ShapeDtypeStruct((2, 32, 1536),...  1.8 us

profile of v2, /device:TPU:8, one launch (start us, length us, event | category | flops | bytes accessed | tf_op | source)
XLA Modules:
  0.0 67.1 jit_solution(9772596959216006088)
XLA Ops:
  0.6 64.7 %compress.1 = (f32[2,32,1536]{2,1,0:T(8,128)}, f32[2,32,384]{2,1,0:T(8,128)}) custom-call(bf16[128,1536]{1,0:T(8,128)(2,1)} %t0_in.1, bf16[256,1536]{1,0:T(8,128)(2,1)} %t1_in.1, bf16[2,256,384]{2,1,0:T(8,128)(2,1)} %g_in.1, bf16[2,1536,384]{2,1,0:T(8,128)(2,1)} %bitcast.4, bf16[2,32,384]{2,1,0:T(8,128)(2,1)} %bitcast.5), custom_call_target="tpu_custom_call" | custom-call | flops 1000000000 | bytes 5000000 | tf_op jit(solution)/shard_map/compress/pallas_call | solution.py:361
  65.3 1.8 %write_out.1 = (f32[2,32,1536]{2,1,0:T(8,128)}, f32[2,32,384]{2,1,0:T(8,128)}) custom-call(f32[2,32,1536]{2,1,0:T(8,128)} %get-tuple-element.6.rb, f32[2,32,384]{2,1,0:T(8,128)} %get-tuple-element.7.cf), custom_call_target="tpu_custom_call" | custom-call | tf_op jit(solution)/shard_map/write_out/pallas_call | solution.py:415

commit v3 on v2

--- a/solution.py
+++ b/solution.py
@@ -52,8 +52,8 @@
 
 
 def kernel(
-    t0_in, t1_in, g_in, f_in, s_in, rb_out, cf_out,
-    t0, t1, g, f, s, u, u_got, g_got, part, rsb, zbuf, pfull, mpart, rs2b, acc2, z2b, mfull, linv, rb, cf,
+    t0_in, t1_in, g_in, f_in, s_in, rb_out, m_out, linv_out,
+    t0, t1, g, f, s, u, u_got, g_got, part, rsb, zbuf, pfull, mpart, rs2b, acc2, z2b, mine, linv, rb,
     load_sem, store_sem, u_sem, g_sem, rs_send, rs_recv, z_sem, ag_send, ag_recv, rs2_sem, z2_sem, ag2_sem,
 ):
     rem, div = lax.rem, lax.div
@@ -117,7 +117,10 @@
     def _():
         pl.semaphore_wait(barrier, 46)
         u_copy.start()
-        g_copy.start()
+
+        @pl.when(c == 0)
+        def _():
+            g_copy.start()
 
     loads[2].wait()
     u1 = halves(dot(s[1], g[1], NT))
@@ -137,7 +140,10 @@
     def _():
         pl.semaphore_wait(barrier, 46)
         u_copy.start()
-        g_copy.start()
+
+        @pl.when(c == 0)
+        def _():
+            g_copy.start()
 
     def send_part(layer):
         other = rem(c + layer, 2)
@@ -207,6 +213,7 @@
         def _():
             reduce_part(1)
 
+        g_copy.start()
         gather_power(1)
 
     @pl.when(c == 0)
@@ -246,8 +253,6 @@
     wait_power(1)
     direct, by_token = products(1, t1)
     put(1, direct + fold(dot(by_token, g[1], NN)))
-    factorize(1)
-    rb_stores[1].start()
 
     g_copy.wait()
     wait_power(0)
@@ -288,6 +293,13 @@
             def _():
                 send(acc2.at[2], z2b.at[z, 0], z2_sem.at[2], z2_sem.at[3], where)
 
+    factorize(1)
+    rb_stores[1].start()
+    linv_store = pltpu.make_async_copy(linv, linv_out, store_sem.at[3])
+    linv_store.start()
+
+    @pl.when(x < 3)
+    def _():
         wait_bytes(z2b.at[pl.ds(0, 7)], z2_sem.at[1])
         wait_bytes(z2b.at[pl.ds(0, 4)], z2_sem.at[3])
         first = z2b[0, 0]
@@ -296,24 +308,19 @@
         second = z2b[gen * 8, 1]
         for slot in range(1, 8):
             second = second + z2b[gen * 8 + slot, 1]
-        mfull[me, 0] = first
-        mfull[me, 1] = second
+        mine[0] = first
+        mine[1] = second
 
         for step in XY_STEPS:
-            send(mfull.at[me], mfull.at[me], ag2_sem.at[0], ag2_sem.at[1], plane(*step, c))
-        wait_bytes(mfull.at[pl.ds(0, 11)], ag2_sem.at[1])
+            send(mine, m_out.at[me], ag2_sem.at[0], ag2_sem.at[1], plane(*step, c))
+        keep = pltpu.make_async_copy(mine, m_out.at[me], store_sem.at[2])
+        keep.start()
+        wait_bytes(m_out.at[pl.ds(0, 11)], ag2_sem.at[1])
+        keep.wait()
 
     @pl.when(x == 3)
     def _():
-        wait_bytes(mfull.at[pl.ds(0, 12)], ag2_sem.at[1])
-
-    for layer in range(2):
-        scaled = linv[layer] * (1.0 / 128.0)
-        for q in range(3):
-            block = mfull[4 * q : 4 * q + 4, layer].reshape(32, 128)
-            cf[layer, :, 128 * q : 128 * q + 128] = dot(scaled, block, NN, HIGHEST)
-    cf_store = pltpu.make_async_copy(cf, cf_out, store_sem.at[2])
-    cf_store.start()
+        wait_bytes(m_out.at[pl.ds(0, 12)], ag2_sem.at[1])
 
     for layer in range(2):
 
@@ -341,31 +348,35 @@
 
     rb_stores[0].wait()
     rb_stores[1].wait()
-    cf_store.wait()
-
-
-def write_out(rb, cf, rb_out, cf_out, sem):
-    copies = [
-        pltpu.make_async_copy(rb, rb_out, sem.at[0]),
-        pltpu.make_async_copy(cf, cf_out, sem.at[1]),
-    ]
-    for copy in copies:
-        copy.start()
-    for copy in copies:
-        copy.wait()
+    linv_store.wait()
+
+
+def write_out(rb, sums, inverse, rb_out, cf_out, cf, sem):
+    rb_copy = pltpu.make_async_copy(rb, rb_out, sem.at[0])
+    rb_copy.start()
+    for layer in range(2):
+        scaled = inverse[layer] * (1.0 / 128.0)
+        for q in range(3):
+            block = sums[4 * q : 4 * q + 4, layer].reshape(32, 128)
+            cf[layer, :, 128 * q : 128 * q + 128] = dot(scaled, block, NN, HIGHEST)
+    cf_copy = pltpu.make_async_copy(cf, cf_out, sem.at[1])
+    cf_copy.start()
+    rb_copy.wait()
+    cf_copy.wait()
 
 
 def local(fresh_tokens, saved_tokens, cotangents, feedback, start_factors):
     anywhere = pl.BlockSpec(memory_space=pl.ANY)
     vmem, dma = pltpu.VMEM, pltpu.SemaphoreType.DMA
-    rb, cf = pl.pallas_call(
+    rb, sums, inverse = pl.pallas_call(
         kernel,
         out_shape=(
             jax.ShapeDtypeStruct((2, 32, 1536), f32),
-            jax.ShapeDtypeStruct((2, 32, 384), f32),
+            jax.ShapeDtypeStruct((12, 2, 8, 128), f32),
+            jax.ShapeDtypeStruct((2, 32, 32), f32),
         ),
         in_specs=[anywhere] * 5,
-        out_specs=(anywhere, anywhere),
+        out_specs=(anywhere, anywhere, anywhere),
         scratch_shapes=[
             vmem((128, 1536), bf16),
             vmem((256, 1536), bf16),
@@ -383,12 +394,11 @@
             vmem((16, 3, 8, 128), f32),
             vmem((3, 8, 128), f32),
             vmem((16, 2, 8, 128), f32),
-            vmem((12, 2, 8, 128), f32),
+            vmem((2, 8, 128), f32),
             vmem((2, 32, 32), f32),
             vmem((2, 32, 1536), f32),
-            vmem((2, 32, 384), f32),
             dma((7,)),
-            dma((3,)),
+            dma((4,)),
             dma((2,)),
             dma((2,)),
             dma((2,)),
@@ -418,11 +428,11 @@
             jax.ShapeDtypeStruct((2, 32, 1536), f32),
             jax.ShapeDtypeStruct((2, 32, 384), f32),
         ),
-        in_specs=[pl.BlockSpec(memory_space=vmem)] * 2,
+        in_specs=[pl.BlockSpec(memory_space=vmem)] * 3,
         out_specs=(anywhere, anywhere),
-        scratch_shapes=[dma((2,))],
+        scratch_shapes=[vmem((2, 32, 384), f32), dma((2,))],
         name="write_out",
-    )(rb, cf)
+    )(rb, sums, inverse)
     return jnp.transpose(rb, (0, 2, 1)), jnp.transpose(cf, (0, 2, 1))
 
 

time: 67.3 us -> 66 us (0.981)
  the two profiles are of different devices: /device:TPU:8 before, /device:TPU:2 now
where the time goes in v3:
time: 66 us; the launch traced here: 65.8 us
  Pallas kernels  65.2 us (99%)
    pallas_call x1, Pallas kernels, local(): pl.pallas_call(kernel, out_shape=(jax.ShapeDtypeStruct((2, 32, 1536), f32...  63.2 us
    pallas_call x1, Pallas kernels, local(): pl.pallas_call(write_out, out_shape=(jax.ShapeDtypeStruct((2, 32, 1536),...  1.96 us

profile of v3, /device:TPU:2, one launch (start us, length us, event | category | flops | bytes accessed | tf_op | source)
XLA Modules:
  0.0 65.8 jit_solution(3876434817740138960)
XLA Ops:
  0.6 63.2 %compress.1 = (f32[2,32,1536]{2,1,0:T(8,128)}, f32[12,2,8,128]{3,2,1,0:T(8,128)}, f32[2,32,32]{2,1,0:T(8,128)}) custom-call(bf16[128,1536]{1,0:T(8,128)(2,1)} %t0_in.1, bf16[256,1536]{1,0:T(8,128)(2,1)} %t1_in.1, bf16[2,256,384]{2,1,0:T(8,128)(2,1)} %g_in.1, bf16[2,1536,384]{2,1,0:T(8,128)(2,1)} %bitcast.4, bf16[2,32,384]{2,1,0:T(8,128)(2,1)} %bitcast.5), custom_call_target="tpu_custom_call" | custom-call | flops 1000000000 | bytes 5000000 | tf_op jit(solution)/shard_map/compress/pallas_call | solution.py:371
  63.8 2.0 %write_out.1 = (f32[2,32,1536]{2,1,0:T(8,128)}, f32[2,32,384]{2,1,0:T(8,128)}) custom-call(f32[2,32,1536]{2,1,0:T(8,128)} %get-tuple-element.7.rb, f32[12,2,8,128]{3,2,1,0:T(8,128)} %get-tuple-element.8.sums, f32[2,32,32]{2,1,0:T(8,128)} %get-tuple-element.9.inverse), custom_call_target="tpu_custom_call" | custom-call | tf_op jit(solution)/shard_map/write_out/pallas_call | solution.py:425

commit v4 on v3

--- a/solution.py
+++ b/solution.py
@@ -54,7 +54,7 @@
 def kernel(
     t0_in, t1_in, g_in, f_in, s_in, rb_out, m_out, linv_out,
     t0, t1, g, f, s, u, u_got, g_got, part, rsb, zbuf, pfull, mpart, rs2b, acc2, z2b, mine, linv, rb,
-    load_sem, store_sem, u_sem, g_sem, rs_send, rs_recv, z_sem, ag_send, ag_recv, rs2_sem, z2_sem, ag2_sem,
+    load_sem, store_sem, u_sem, g_sem, rs_send, rs_recv, z_sem, ag_send, ag_recv, pair_sem, rs2_sem, z2_sem, ag2_sem,
 ):
     rem, div = lax.rem, lax.div
     dp, c, gen = lax.axis_index("dp"), lax.axis_index("mp"), lax.axis_index("gen")
@@ -172,22 +172,24 @@
         for slot in range(1, 16):
             total = total + zbuf[slot]
         pfull[layer, me] = total
-        for dx, dy in XY_STEPS + [(0, 0)]:
-            for k in range(2):
-                if dx + dy + k > 0:
-                    send(
-                        pfull.at[layer, me], pfull.at[layer, me],
-                        ag_send, ag_recv.at[layer], plane(dx, dy, cs[k]),
-                    )
+        for step in XY_STEPS:
+            send(pfull.at[layer, me], pfull.at[layer, me], ag_send, ag_recv, plane(*step, c))
 
     def wait_power(layer):
+        forward = pltpu.make_async_remote_copy(
+            src_ref=pfull.at[layer], dst_ref=pfull.at[layer],
+            send_sem=pair_sem.at[0], recv_sem=pair_sem.at[1],
+            device_id=plane(0, 0, cs[1]), device_id_type=MESH,
+        )
+
         @pl.when(c == layer)
         def _():
-            wait_bytes(pfull.at[layer, pl.ds(0, 15)], ag_recv.at[layer])
+            wait_bytes(pfull.at[layer, pl.ds(0, 15)], ag_recv)
+            forward.start()
 
         @pl.when(c != layer)
         def _():
-            wait_bytes(pfull.at[layer, pl.ds(0, 16)], ag_recv.at[layer])
+            forward.wait_recv()
 
     def power_block(layer, q):
         return pfull[layer, 4 * q : 4 * q + 4].reshape(32, 384)
@@ -333,7 +335,8 @@
             wait_bytes(part.at[layer, pl.ds(0, 16)], rs_send.at[layer])
 
     wait_bytes(zbuf.at[pl.ds(0, 15)], z_sem.at[0])
-    wait_bytes(rsb.at[pl.ds(0, 31)], ag_send)
+    wait_bytes(rsb.at[pl.ds(0, 15)], ag_send)
+    wait_bytes(rsb.at[pl.ds(0, 16)], pair_sem.at[0])
 
     @pl.when(x < 3)
     def _():
@@ -351,18 +354,27 @@
     linv_store.wait()
 
 
-def write_out(rb, sums, inverse, rb_out, cf_out, cf, sem):
-    rb_copy = pltpu.make_async_copy(rb, rb_out, sem.at[0])
-    rb_copy.start()
+def write_out(rb_in, sums_in, inverse_in, rb_out, cf_out, rb, sums, inverse, cf, sem):
+    sums_load = pltpu.make_async_copy(sums_in, sums, sem.at[0])
+    inverse_load = pltpu.make_async_copy(inverse_in, inverse, sem.at[1])
+    rb_load = pltpu.make_async_copy(rb_in, rb, sem.at[2])
+    rb_copy = pltpu.make_async_copy(rb, rb_out, sem.at[3])
+    cf_copy = pltpu.make_async_copy(cf, cf_out, sem.at[4])
+    sums_load.start()
+    inverse_load.start()
+    rb_load.start()
+    sums_load.wait()
+    inverse_load.wait()
     for layer in range(2):
         scaled = inverse[layer] * (1.0 / 128.0)
         for q in range(3):
             block = sums[4 * q : 4 * q + 4, layer].reshape(32, 128)
             cf[layer, :, 128 * q : 128 * q + 128] = dot(scaled, block, NN, HIGHEST)
-    cf_copy = pltpu.make_async_copy(cf, cf_out, sem.at[1])
     cf_copy.start()
+    rb_load.wait()
+    rb_copy.start()
+    cf_copy.wait()
     rb_copy.wait()
-    cf_copy.wait()
 
 
 def local(fresh_tokens, saved_tokens, cotangents, feedback, start_factors):
@@ -405,6 +417,7 @@
             dma,
             dma((2,)),
             dma,
+            dma,
             dma((2,)),
             dma((2,)),
             dma((4,)),
@@ -428,9 +441,15 @@
             jax.ShapeDtypeStruct((2, 32, 1536), f32),
             jax.ShapeDtypeStruct((2, 32, 384), f32),
         ),
-        in_specs=[pl.BlockSpec(memory_space=vmem)] * 3,
+        in_specs=[anywhere] * 3,
         out_specs=(anywhere, anywhere),
-        scratch_shapes=[vmem((2, 32, 384), f32), dma((2,))],
+        scratch_shapes=[
+            vmem((2, 32, 1536), f32),
+            vmem((12, 2, 8, 128), f32),
+            vmem((2, 32, 32), f32),
+            vmem((2, 32, 384), f32),
+            dma((5,)),
+        ],
         name="write_out",
     )(rb, sums, inverse)
     return jnp.transpose(rb, (0, 2, 1)), jnp.transpose(cf, (0, 2, 1))

time: 66 us -> 65.7 us (level)
  no operation moved by 1% of the time
where the time goes in v4:
time: 65.7 us; the launch traced here: 65.6 us
  Pallas kernels  64.9 us (99%)
    pallas_call x1, Pallas kernels, local(): pl.pallas_call(kernel, out_shape=(jax.ShapeDtypeStruct((2, 32, 1536), f32...  63 us
    pallas_call x1, Pallas kernels, local(): pl.pallas_call(write_out, out_shape=(jax.ShapeDtypeStruct((2, 32, 1536),...  1.97 us

profile of v4, /device:TPU:2, one launch (start us, length us, event | category | flops | bytes accessed | tf_op | source)
XLA Modules:
  0.0 65.6 jit_solution(4955410515205646174)
XLA Ops:
  0.6 63.0 %compress.1 = (f32[2,32,1536]{2,1,0:T(8,128)}, f32[12,2,8,128]{3,2,1,0:T(8,128)}, f32[2,32,32]{2,1,0:T(8,128)}) custom-call(bf16[128,1536]{1,0:T(8,128)(2,1)} %t0_in.1, bf16[256,1536]{1,0:T(8,128)(2,1)} %t1_in.1, bf16[2,256,384]{2,1,0:T(8,128)(2,1)} %g_in.1, bf16[2,1536,384]{2,1,0:T(8,128)(2,1)} %bitcast.4, bf16[2,32,384]{2,1,0:T(8,128)(2,1)} %bitcast.5), custom_call_target="tpu_custom_call" | custom-call | flops 1000000000 | bytes 5000000 | tf_op jit(solution)/shard_map/compress/pallas_call | solution.py:383
  63.6 2.0 %write_out.1 = (f32[2,32,1536]{2,1,0:T(8,128)}, f32[2,32,384]{2,1,0:T(8,128)}) custom-call(f32[2,32,1536]{2,1,0:T(8,128)} %get-tuple-element.7.rb_in, f32[12,2,8,128]{3,2,1,0:T(8,128)} %get-tuple-element.8.sums_in, f32[2,32,32]{2,1,0:T(8,128)} %get-tuple-element.9.inverse_in), custom_call_target="tpu_custom_call" | custom-call | tf_op jit(solution)/shard_map/write_out/pallas_call | solution.py:438

commit v5 on v4

--- a/solution.py
+++ b/solution.py
@@ -90,13 +90,13 @@
         pltpu.make_async_copy(f_in.at[0], f.at[0], load_sem.at[5]),
         pltpu.make_async_copy(t0_in, t0, load_sem.at[6]),
     ]
-    for load in loads:
-        load.start()
-
     barrier = pltpu.get_barrier_semaphore()
     peers = [along(dz) for dz in Z_STEPS] + [plane(*step, cs[k]) for step in XY_STEPS for k in range(2)]
     for peer in peers + [plane(0, 0, cs[1])]:
         pl.semaphore_signal(barrier, inc=1, device_id=peer, device_id_type=MESH)
+
+    for load in loads:
+        load.start()
 
     loads[0].wait()
     loads[1].wait()

time: 65.7 us -> 65.7 us (level)
  no operation moved by 1% of the time
where the time goes in v5:
time: 65.7 us; the launch traced here: 65.6 us
  Pallas kernels  64.9 us (99%)
    pallas_call x1, Pallas kernels, local(): pl.pallas_call(kernel, out_shape=(jax.ShapeDtypeStruct((2, 32, 1536), f32...  63 us
    pallas_call x1, Pallas kernels, local(): pl.pallas_call(write_out, out_shape=(jax.ShapeDtypeStruct((2, 32, 1536),...  1.97 us

profile of v5, /device:TPU:2, one launch (start us, length us, event | category | flops | bytes accessed | tf_op | source)
XLA Modules:
  0.0 65.6 jit_solution(11356463132030265179)
XLA Ops:
  0.6 63.0 %compress.1 = (f32[2,32,1536]{2,1,0:T(8,128)}, f32[12,2,8,128]{3,2,1,0:T(8,128)}, f32[2,32,32]{2,1,0:T(8,128)}) custom-call(bf16[128,1536]{1,0:T(8,128)(2,1)} %t0_in.1, bf16[256,1536]{1,0:T(8,128)(2,1)} %t1_in.1, bf16[2,256,384]{2,1,0:T(8,128)(2,1)} %g_in.1, bf16[2,1536,384]{2,1,0:T(8,128)(2,1)} %bitcast.4, bf16[2,32,384]{2,1,0:T(8,128)(2,1)} %bitcast.5), custom_call_target="tpu_custom_call" | custom-call | flops 1000000000 | bytes 5000000 | tf_op jit(solution)/shard_map/compress/pallas_call | solution.py:383
  63.6 2.0 %write_out.1 = (f32[2,32,1536]{2,1,0:T(8,128)}, f32[2,32,384]{2,1,0:T(8,128)}) custom-call(f32[2,32,1536]{2,1,0:T(8,128)} %get-tuple-element.7.rb_in, f32[12,2,8,128]{3,2,1,0:T(8,128)} %get-tuple-element.8.sums_in, f32[2,32,32]{2,1,0:T(8,128)} %get-tuple-element.9.inverse_in), custom_call_target="tpu_custom_call" | custom-call | tf_op jit(solution)/shard_map/write_out/pallas_call | solution.py:438
